TPU v7x, 1024 devices: a whole 4x4x32 slice. The times are simulated.
1024 devices in a mesh: dp: 64 (over z, core), tensor: 16 (over x, y).
Axes of the slice: x: 4, y: 4, z: 32, core: 2. Of those that a mesh axis runs over, the one named last changes fastest.
Arguments:
- x_quant: bfloat16 [384, 8192], P('tensor', 'dp'), may hold values from -6 to 6
- x_scale: float32 [16, 64], P('tensor', 'dp'), may hold values from 0.25 to 4
- x_outlier: int32 [16, 64], P('tensor', 'dp'), may hold values 0 or 1
- x_correction: bfloat16 [384, 8192], P('tensor', 'dp'), may hold values from -12 to 12
- g_quant: bfloat16 [384, 8192], P('tensor', 'dp'), may hold values from -6 to 6
- g_scale: float32 [16, 64], P('tensor', 'dp'), may hold values from 0.25 to 4
- g_outlier: int32 [16, 64], P('tensor', 'dp'), may hold values 0 or 1
- g_correction: bfloat16 [384, 8192], P('tensor', 'dp'), may hold values from -12 to 12
- gate_pre: bfloat16 [384, 26624], P('dp', 'tensor'), may hold values from -8 to 8
- up_pre: bfloat16 [384, 26624], P('dp', 'tensor'), may hold values from -6 to 6
- w_gate: bfloat16 [8192, 26624], P('dp', 'tensor'), may hold values from -0.0625 to 0.0625
- w_up: bfloat16 [8192, 26624], P('dp', 'tensor'), may hold values from -0.0625 to 0.0625
- w_down: bfloat16 [26624, 8192], P('tensor', 'dp'), may hold values from -0.0625 to 0.0625
Outputs:
- grad_input: bfloat16 [384, 8192], P('tensor', 'dp')
- grad_gate_weight: bfloat16 [8192, 26624], P('dp', 'tensor')
- grad_up_weight: bfloat16 [8192, 26624], P('dp', 'tensor')
- grad_down_weight: bfloat16 [26624, 8192], P('tensor', 'dp')
All inputs are finite; a program needn't handle non-finite values. No bound on the sum of `x_outlier` or of `g_outlier` on one device may be relied on, other than what follows from the above.
Results may differ from a plain program's by a relative error of at most 0.0064.
Values may be sent and summed in bfloat16 or wider, within the bound.
A program may use at most 32 MiB of HBM per device.

v0:
```python
import jax
import jax.numpy as jnp
from jax import lax
from jax.sharding import PartitionSpec as P

BLK_C = 128


def dequantize(quant, block_scale, outlier, correction):
    scale_cols = jnp.repeat(block_scale, BLK_C, axis=1)
    outlier_cols = jnp.repeat(outlier.astype(jnp.float32), BLK_C, axis=1)
    values = scale_cols * quant.astype(jnp.float32) + outlier_cols * correction.astype(jnp.float32)
    return values.astype(jnp.bfloat16)


def contract_rows(left, right):
    return lax.dot_general(
        left, right, (((0,), (0,)), ((), ())), preferred_element_type=jnp.float32
    )


def contract_cols(left, right):
    return lax.dot_general(
        left, right, (((1,), (1,)), ((), ())), preferred_element_type=jnp.float32
    )


def on_device(
    x_quant,
    x_scale,
    x_outlier,
    x_correction,
    g_quant,
    g_scale,
    g_outlier,
    g_correction,
    gate_pre,
    up_pre,
    w_gate,
    w_up,
    w_down,
):
    inputs = dequantize(x_quant, x_scale, x_outlier, x_correction)
    out_grad = dequantize(g_quant, g_scale, g_outlier, g_correction)
    inputs_all, out_grad_all = (
        lax.all_gather(inputs, "tensor", axis=0, tiled=True),
        lax.all_gather(out_grad, "tensor", axis=0, tiled=True),
    )
    grad_rows = out_grad_all
    hidden_grad = lax.psum_scatter(
        contract_cols(grad_rows, w_down), "dp", scatter_dimension=0, tiled=True
    )
    gate_val = gate_pre.astype(jnp.float32)
    up_val = up_pre.astype(jnp.float32)
    sigmoid_gate = jax.nn.sigmoid(gate_val)
    silu_gate = gate_val * sigmoid_gate
    up_grad = (hidden_grad * silu_gate).astype(jnp.bfloat16)
    gate_grad = (
        hidden_grad * up_val * sigmoid_gate * (1.0 + gate_val * (1.0 - sigmoid_gate))
    ).astype(jnp.bfloat16)
    gate_rows = lax.all_gather(gate_pre, "dp", axis=0, tiled=True).astype(jnp.float32)
    rebuilt = (
        gate_rows
        * jax.nn.sigmoid(gate_rows)
        * lax.all_gather(up_pre, "dp", axis=0, tiled=True).astype(jnp.float32)
    ).astype(jnp.bfloat16)
    gate_piece = lax.all_gather(gate_grad, "dp", axis=0, tiled=True)
    up_piece = lax.all_gather(up_grad, "dp", axis=0, tiled=True)
    grad_rows = out_grad_all
    down_total = contract_rows(rebuilt, grad_rows)
    gate_total = contract_rows(inputs_all, gate_piece)
    up_total = contract_rows(inputs_all, up_piece)
    input_part = contract_cols(gate_piece, w_gate) + contract_cols(up_piece, w_up)
    grad_input = lax.psum_scatter(input_part, "tensor", scatter_dimension=0, tiled=True).astype(
        jnp.bfloat16
    )
    return (
        grad_input,
        gate_total.astype(jnp.bfloat16),
        up_total.astype(jnp.bfloat16),
        down_total.astype(jnp.bfloat16),
    )


def solution(mesh):
    return jax.shard_map(
        on_device,
        mesh=mesh,
        in_specs=(
            P("tensor", "dp"),
            P("tensor", "dp"),
            P("tensor", "dp"),
            P("tensor", "dp"),
            P("tensor", "dp"),
            P("tensor", "dp"),
            P("tensor", "dp"),
            P("tensor", "dp"),
            P("dp", "tensor"),
            P("dp", "tensor"),
            P("dp", "tensor"),
            P("dp", "tensor"),
            P("tensor", "dp"),
        ),
        out_specs=(P("tensor", "dp"), P("dp", "tensor"), P("dp", "tensor"), P("tensor", "dp")),
        check_vma=False,
    )
```

profile of v0, /device:TPU:1, one launch (start us, length us, event | category | flops | bytes accessed | tf_op | source)
XLA Modules:
  0.0 1098.1 jit_solution(4096671697476928622)
XLA Ops:
  7.2 0.0 copy-start
  7.2 0.0 all-reduce.4.cloned.1.call-start
  8.6 0.7 add_convert_fusion.1
  9.3 19.3 %all_gather.18 = bf16[384,128]{1,0:T(8,128)(2,1)S(1)} all-gather(bf16[24,128]{1,0:T(8,128)(2,1)S(1)} %add_convert_fusion.1), channel_id=1, replica_groups=mesh['dp'=64,'tensor'=16] {'tensor'}, dimensions={0}, use_global_device_ids=true | all-gather | bytes 104448 | tf_op jit(solution)/shard_map/all_gather | solution.py:47
  28.5 0.0 copy-done
  28.5 2.0 fusion.11
  30.6 0.0 copy-start.2
  30.6 0.0 copy-start.3
  30.6 0.0 copy-start.4
  30.6 0.0 copy-start.5
  30.6 0.0 all-reduce.4.cloned.1.call-update
  30.6 0.0 all-gather.13.cloned.1.call-start
  30.7 0.7 all-gather.13.cloned.1.call-update
  31.4 0.0 all-gather.15.cloned.1.call-start
  31.4 0.7 all-gather.15.cloned.1.call-update
  32.1 0.0 all-gather.9.cloned.1.call-start
  32.2 1.3 dynamic-slice
  34.1 420.1 %all-reduce.4.cloned.1.call-done = f32[384,1664]{1,0:T(8,128)} async-done(((f32[384,1664]{1,0:T(8,128)}), f32[384,1664]{1,0:T(8,128)}) %all-reduce.4.cloned.1.call-update) | async-done | bytes 2555920
  454.2 0.0 copy-done.2
  454.2 0.0 copy-done.3
  454.2 1.6 fusion.8
  455.8 0.0 all-gather.9.cloned.1.call-update
  455.8 0.0 all-gather.11.cloned.1.call-start
  455.8 0.5 all-gather.11.cloned.1.call-update
  456.4 0.0 reduce-scatter.4.cloned.1.call-start
  457.7 0.0 copy-done.4
  457.7 0.0 copy-done.5
  457.7 18.1 %all_gather.21 = bf16[384,128]{1,0:T(8,128)(2,1)S(1)} all-gather(bf16[24,128]{1,0:T(8,128)(2,1)S(1)} %add_convert_fusion), channel_id=1, replica_groups=mesh['dp'=64,'tensor'=16] {'tensor'}, dimensions={0}, use_global_device_ids=true | all-gather | bytes 104448 | tf_op jit(solution)/shard_map/all_gather | solution.py:46
  475.9 117.9 %all-gather.13.cloned.1.call-done = bf16[64,6,1664]{2,1,0:T(8,128)(2,1)} async-done(((bf16[1,6,1664]{2,1,0:T(8,128)(2,1)}), bf16[64,6,1664]{2,1,0:T(8,128)(2,1)}) %all-gather.13.cloned.1.call-update) | async-done | bytes 1277968 | tf_op jit(solution)/shard_map/all_gather | solution.py:61
  593.8 2.3 reshape.24
  596.1 128.7 %all-gather.15.cloned.1.call-done = bf16[64,6,1664]{2,1,0:T(8,128)(2,1)} async-done(((bf16[1,6,1664]{2,1,0:T(8,128)(2,1)}), bf16[64,6,1664]{2,1,0:T(8,128)(2,1)}) %all-gather.15.cloned.1.call-update) | async-done | bytes 1277968 | tf_op jit(solution)/shard_map/all_gather | solution.py:65
  724.8 3.5 reshape.25
  728.3 3.4 convolution_convert_fusion
  731.6 0.0 copy-start.1
  731.6 124.7 %all-gather.9.cloned.1.call-done = bf16[64,6,1664]{2,1,0:T(8,128)(2,1)} async-done(((bf16[1,6,1664]{2,1,0:T(8,128)(2,1)}), bf16[64,6,1664]{2,1,0:T(8,128)(2,1)}) %all-gather.9.cloned.1.call-update) | async-done | bytes 1277968 | tf_op jit(solution)/shard_map/all_gather | solution.py:67
  856.3 2.4 reshape.17
  858.7 0.0 copy-done.1
  858.7 0.5 fusion.12
  859.2 128.6 %all-gather.11.cloned.1.call-done = bf16[64,6,1664]{2,1,0:T(8,128)(2,1)} async-done(((bf16[1,6,1664]{2,1,0:T(8,128)(2,1)}), bf16[64,6,1664]{2,1,0:T(8,128)(2,1)}) %all-gather.11.cloned.1.call-update) | async-done | bytes 1277968 | tf_op jit(solution)/shard_map/all_gather | solution.py:68
  987.8 2.4 reshape.19
  990.2 2.2 convolution_add_fusion
  992.4 0.0 reduce-scatter.4.cloned.1.call-update
  992.4 1.2 convolution_convert_fusion.2
  993.6 1.2 convolution_convert_fusion.1
  994.8 95.2 %reduce-scatter.4.cloned.1.call-done = f32[24,128]{1,0:T(8,128)} async-done(((f32[384,128]{1,0:T(8,128)}), f32[24,128]{1,0:T(8,128)}) %reduce-scatter.4.cloned.1.call-update) | async-done | bytes 12304
  1089.9 1.3 convert_element_type.70
  (1 shorter events, 0.0 us)
Async XLA Ops:
  7.2 21.4 %copy-start = (bf16[1664,128]{1,0:T(8,128)(2,1)S(1)}, bf16[1664,128]{1,0:T(8,128)(2,1)}, u32[]{:S(2)}) copy-start(bf16[1664,128]{1,0:T(8,128)(2,1)} %param.25) | copy-start | bytes 1277956
  7.2 447.0 %all-reduce.4.cloned.1.call-start = ((), (), s32[]{:S(2)}) async-start(), calls=%async_computation.5 | async-start | bytes 5111808
  30.6 423.6 %copy-start.2 = (bf16[6,1664]{1,0:T(8,128)(2,1)S(1)}, bf16[6,1664]{1,0:T(8,128)(2,1)}, u32[]{:S(2)}) copy-start(bf16[6,1664]{1,0:T(8,128)(2,1)} %param.21) | copy-start | bytes 59908
  30.6 423.6 %copy-start.3 = (bf16[6,1664]{1,0:T(8,128)(2,1)S(1)}, bf16[6,1664]{1,0:T(8,128)(2,1)}, u32[]{:S(2)}) copy-start(bf16[6,1664]{1,0:T(8,128)(2,1)} %param.22) | copy-start | bytes 59908
  30.6 427.1 %copy-start.4 = (bf16[24,128]{1,0:T(8,128)(2,1)S(1)}, bf16[24,128]{1,0:T(8,128)(2,1)}, u32[]{:S(2)}) copy-start(bf16[24,128]{1,0:T(8,128)(2,1)} %param.16) | copy-start | bytes 18436
  30.6 427.1 %copy-start.5 = (bf16[24,128]{1,0:T(8,128)(2,1)S(1)}, bf16[24,128]{1,0:T(8,128)(2,1)}, u32[]{:S(2)}) copy-start(bf16[24,128]{1,0:T(8,128)(2,1)} %param.13) | copy-start | bytes 18436
  30.6 563.2 %all-gather.13.cloned.1.call-start = ((), (), s32[]{:S(2)}) async-start(), calls=%async_computation.3 | async-start | bytes 1730560 | tf_op jit(solution)/shard_map/all_gather | solution.py:61
  31.4 693.4 %all-gather.15.cloned.1.call-start = ((), (), s32[]{:S(2)}) async-start(), calls=%async_computation.4 | async-start | bytes 1730560 | tf_op jit(solution)/shard_map/all_gather | solution.py:65
  32.1 824.2 %all-gather.9.cloned.1.call-start = ((), (), s32[]{:S(2)}) async-start(), calls=%async_computation.1 | async-start | bytes 1730560 | tf_op jit(solution)/shard_map/all_gather | solution.py:67
  455.8 532.0 %all-gather.11.cloned.1.call-start = ((), (), s32[]{:S(2)}) async-start(), calls=%async_computation.2 | async-start | bytes 1730560 | tf_op jit(solution)/shard_map/all_gather | solution.py:68
  456.4 633.6 %reduce-scatter.4.cloned.1.call-start = ((), (), s32[]{:S(2)}) async-start(), calls=%async_computation.6 | async-start | bytes 208896
  731.6 127.1 %copy-start.1 = (bf16[128,1664]{1,0:T(8,128)(2,1)S(1)}, bf16[128,1664]{1,0:T(8,128)(2,1)}, u32[]{:S(2)}) copy-start(bf16[128,1664]{1,0:T(8,128)(2,1)} %param.23) | copy-start | bytes 1277956
Sparse Core Ops, SparseCore 0:
  30.7 423.4 all-reduce.3
  457.3 136.4 all-gather.12
  596.8 127.9 all-gather.14
  728.3 127.9 all-gather.8
  859.8 127.9 all-gather.10
  993.7 96.2 reduce-scatter.3
where the time goes:
time: 1100 us
  waiting for transfers between devices  1020 us (93%)
  blocking collectives  37.4 us (3%)
  between operations  17.5 us (2%)
  local copies, waits for them, and re-layouts  11.9 us (1%)
    unnamed x8, waiting for transfers between devices  517 us
    all_gather x1, waiting for transfers between devices, on_device(): lax.all_gather(up_pre, 'dp', axis=0, tiled=True).astype(jnp.float32)  129 us
    all_gather x1, waiting for transfers between devices, on_device(): up_piece = lax.all_gather(up_grad, 'dp', axis=0, tiled=True)  129 us
    all_gather x1, waiting for transfers between devices, on_device(): gate_piece = lax.all_gather(gate_grad, 'dp', axis=0, tiled=True)  125 us
    all_gather x1, waiting for transfers between devices, on_device(): lax.all_gather(gate_pre, 'dp', axis=0, tiled=True).astype(jnp.float32)  118 us
  transfers between devices with their start and end apart: 6, of which 6 were waited for; matrix products, arithmetic and copies ran while one was open for 2% of the time, Pallas kernels for 0%

commit v1 on v0

v1 whole, which is shorter than its diff:
```python
import jax
import jax.numpy as jnp
from jax import lax
from jax.experimental import pallas as pl
from jax.experimental.pallas import tpu as pltpu
from jax.sharding import PartitionSpec as P

MESH = pl.DeviceIdType.MESH
F32, BF16 = jnp.float32, jnp.bfloat16

NZ, STRIDE = 32, 4
NK = NZ // STRIDE
NT = 16
J = 13
ROWS = 192
CH = 80
FLAT = NZ * CH
CLS = NK * CH
HALF = CLS // 2
GCH = 2 * CH
GCLS = NK * GCH
GHALF = GCLS // 2
XY = 48


def rows_of(start, size, align=16):
    return pl.ds(pl.multiple_of(start, align), size)


def kernel(
    xs, xo, gs, go, xq, xc, gq, gc, gate, up, wd, wg, wu,
    gin, dgate, dup, ddown,
    xyb, tmp48, u4, xg, xot, og2, ogall, wd2, wgv, wuv,
    gpack, gbuf, tt, tg, tu, coef_a, coef_b, hid_o, hid_s,
    hf, hp, r1a, r1b, r1h, sb, sown, r2, ha,
    gu_o, gu_s, part, rs_src, rs_dst, fin, o_gate, o_up, o_down,
    loc_sem, sib_s, sib_r, xy_s, xy_r, gch_s, gch_r, glo_s, glo_r,
    r1_s, r1_r, r2_s, r2_r, a1_s, a1_r, a2_s, a2_r, rs_s, rs_r,
):
    dp, t = lax.axis_index("dp"), lax.axis_index("tensor")
    z, c = dp // 2, lax.rem(dp, 2)
    k0, cls = z // STRIDE, lax.rem(z, STRIDE)

    def zdev(d):
        return (lax.rem(dp + 2 * d + 2 * NZ, 2 * NZ), t)

    def tdev(i):
        return (dp, lax.rem(t + i, NT))

    sib = (dp + 1 - 2 * c, t)

    def rcopy(src, dst, ss, rs, dev):
        return pltpu.make_async_remote_copy(
            src_ref=src, dst_ref=dst, send_sem=ss, recv_sem=rs, device_id=dev, device_id_type=MESH
        )

    barrier = pltpu.get_barrier_semaphore()
    peers = [zdev(d) for d in (1, -1, 2, -2)] + [zdev(STRIDE * i) for i in range(1, NK)]
    peers += [sib] + [tdev(i) for i in range(1, NT)]
    for peer in peers:
        pl.semaphore_signal(barrier, inc=1, device_id=peer, device_id_type=MESH)

    loc = [
        pltpu.make_async_copy(wd, wd2.at[:, pl.ds(0, 128)], loc_sem.at[0]),
        pltpu.make_async_copy(wg, wgv, loc_sem.at[1]),
        pltpu.make_async_copy(wu, wuv, loc_sem.at[2]),
    ]
    for copy in loc:
        copy.start()

    fin[0] = xs[0, 0] * xq[...].astype(F32) + xo[0, 0].astype(F32) * xc[...].astype(F32)
    fin[1] = gs[0, 0] * gq[...].astype(F32) + go[0, 0].astype(F32) * gc[...].astype(F32)
    for a in range(2):
        for p in range(2):
            for h in range(2):
                tmp48[0, 24 * a + 12 * p + 6 * h : 24 * a + 12 * p + 6 * h + 6, :] = fin[
                    a, 12 * h + 6 * p : 12 * h + 6 * p + 6, :
                ]
    xyb[t] = tmp48[0].astype(BF16)

    gpack[...] = jnp.zeros_like(gpack)
    gate_val, up_val = gate[...].astype(F32), up[...].astype(F32)
    for j in range(J):
        gpack[6 * j : 6 * j + 6, :] = gate_val[:, 128 * j : 128 * j + 128]
        gpack[CH + 6 * j : CH + 6 * j + 6, :] = up_val[:, 128 * j : 128 * j + 128]

    def gslot(k):
        return gbuf.at[rows_of(GCLS * cls + GCH * k, GCH)]

    gbuf[rows_of(GCLS * cls + GCH * k0, GCH), :] = gpack[...].astype(BF16)
    pl.semaphore_wait(barrier, len(peers))

    xy = [
        rcopy(xyb.at[t], xyb.at[t], xy_s.at[i - 1], xy_r.at[i - 1], tdev(i))
        for i in (10, 5, 6, 7, 9, 11, 2, 8, 14, 13, 3, 1, 15, 4, 12)
    ]
    for copy in xy:
        copy.start()
    wd_copy = rcopy(wd, wd2.at[:, pl.ds(128, 128)], sib_s.at[0], sib_r.at[0], sib)
    wd_copy.start()

    def chain(s):
        kr, kl = lax.rem(k0 + NK - s + 1, NK), lax.rem(k0 + s - 1, NK)
        out = [rcopy(gslot(kr), gslot(kr), gch_s.at[s - 1], gch_r.at[s - 1], zdev(STRIDE))]
        if s < NK // 2:
            at = NK // 2 + s - 1
            out.append(rcopy(gslot(kl), gslot(kl), gch_s.at[at], gch_r.at[at], zdev(-STRIDE)))
        return out

    chains = [chain(s) for s in range(1, NK // 2 + 1)]
    for copy in chains[0]:
        copy.start()

    def chain_step(s):
        for copy in chains[s - 1]:
            copy.wait_recv()
        for copy in chains[s]:
            copy.start()

    for copy in xy:
        copy.wait_recv()
    for i in range(NT):
        tmp48[i % 4] = xyb[i].astype(F32)
        for a in range(4):
            u4[a, 12 * i : 12 * i + 12, :] = tmp48[i % 4, 12 * a : 12 * a + 12, :]
    for a in range(4):
        xg[a] = u4[a].astype(BF16)
    og_copy = rcopy(xg.at[3 - c], og2.at[:, pl.ds(128, 128)], sib_s.at[1], sib_r.at[1], sib)
    og_copy.start()
    og2[:, 0:128] = xg[2 + c]
    ogall[0:ROWS, :] = xg[2 + c]
    ogall[ROWS : 2 * ROWS, :] = xg[3 - c]
    tx = jnp.concatenate([u4[c], u4[1 - c]], axis=0)
    xot[...] = jnp.transpose(tx).astype(BF16)
    loc[0].wait()
    wd_copy.wait_recv()
    og_copy.wait_recv()

    hp[J * ROWS : FLAT, :] = jnp.zeros((FLAT - J * ROWS, 128), BF16)
    hf[J * ROWS : FLAT, :] = jnp.zeros((FLAT - J * ROWS, 128), F32)
    og_val = og2[...]
    for j in range(J):
        val = lax.dot_general(
            og_val, wd2[128 * j : 128 * j + 128, :], (((1,), (1,)), ((), ())),
            preferred_element_type=F32,
        )
        hf[ROWS * j : ROWS * (j + 1), :] = val
        hp[ROWS * j : ROWS * (j + 1), :] = val.astype(BF16)

    def near(d):
        return lax.rem(cls + d + STRIDE, STRIDE)

    def window(src, dst, cls_rows, sems_s, sems_r, towards):
        half = cls_rows // 2
        out = []
        for n, (d, off, size) in enumerate(
            ((2, 0, half), (-2, half, half), (1, 0, cls_rows), (-1, 0, cls_rows))
        ):
            base = cls_rows * (near(d) if towards else cls) + off
            view = src.at[rows_of(base, size)]
            land = view if dst is None else dst[n]
            out.append(rcopy(view, land, sems_s.at[n], sems_r.at[n], zdev(d)))
        return out

    r1 = window(hp, (r1h.at[rows_of(0, HALF)], r1h.at[rows_of(HALF, HALF)], r1a, r1b), CLS, r1_s, r1_r, True)
    for copy in r1:
        copy.start()
    chain_step(1)
    chain_step(2)
    for copy in r1:
        copy.wait_recv()

    def sum_window(i, _):
        at = rows_of(CH * i, CH)
        own = hf[rows_of(CLS * cls + CH * i, CH), :]
        total = own + r1a[at, :].astype(F32) + r1b[at, :].astype(F32) + r1h[at, :].astype(F32)
        sown[at, :] = total
        sb[at, :] = total.astype(BF16)
        return 0

    lax.fori_loop(0, NK, sum_window, 0)

    far = (4, 3, 5, 2, 6, 1, 7)

    def other(i):
        return lax.rem(k0 + i, NK)

    r2c = [
        rcopy(
            sb.at[rows_of(CH * other(i), CH)], r2.at[k0], r2_s.at[i - 1], r2_r.at[i - 1],
            zdev(STRIDE * i),
        )
        for i in far
    ]
    for copy in r2c:
        copy.start()
    chain_step(3)
    for copy in chains[3]:
        copy.wait_recv()
    glo = window(gbuf, None, GCLS, glo_s, glo_r, False)
    for copy in glo:
        copy.start()

    for copy in r2c:
        copy.wait_recv()
    total = sown[rows_of(CH * k0, CH), :]
    for i in range(1, NK):
        total = total + r2[other(i)].astype(F32)
    own_at = rows_of(CLS * cls + CH * k0, CH)
    ha[own_at, :] = total.astype(BF16)
    a1 = [
        rcopy(ha.at[own_at], ha.at[own_at], a1_s.at[i - 1], a1_r.at[i - 1], zdev(STRIDE * i))
        for i in far
    ]
    for copy in a1:
        copy.start()

    for copy in glo:
        copy.wait_recv()
    coef_a[J * ROWS : FLAT, :] = jnp.zeros((FLAT - J * ROWS, 128), F32)
    coef_b[J * ROWS : FLAT, :] = jnp.zeros((FLAT - J * ROWS, 128), F32)

    def factors(m, _):
        for q in range(8):
            start = GCLS * (q % STRIDE) + GCH * (q // STRIDE) + 2 * GCH * m
            tt[q] = gbuf[rows_of(start, GCH), :].astype(F32)
            for j in range(J):
                tg[j, 6 * q : 6 * q + 6, :] = tt[q, 6 * j : 6 * j + 6, :]
                tu[j, 6 * q : 6 * q + 6, :] = tt[q, CH + 6 * j : CH + 6 * j + 6, :]

        def tile(j, _):
            g, u = tg[j], tu[j]
            s = 1.0 / (1.0 + jnp.exp(-g))
            silu = g * s
            at = rows_of(ROWS * j + 48 * m, 48)
            hid_o[at, :] = (silu * u).astype(BF16)
            coef_a[at, :] = silu
            coef_b[at, :] = u * s * (1.0 + g * (1.0 - s))
            return 0

        lax.fori_loop(0, J, tile, 0)
        return 0

    lax.fori_loop(0, 4, factors, 0)
    hid_copy = rcopy(hid_o, hid_s, sib_s.at[2], sib_r.at[2], sib)
    hid_copy.start()
    hid_copy.wait_recv()

    def down(j, _):
        at = rows_of(ROWS * j, ROWS)
        both = jnp.concatenate([hid_o[at, :], hid_s[at, :]], axis=0)
        val = lax.dot_general(
            both, ogall[...], (((0,), (0,)), ((), ())), preferred_element_type=F32
        )
        o_down[rows_of(128 * j, 128), :] = val.astype(BF16)
        return 0

    lax.fori_loop(0, J, down, 0)
    out_down = pltpu.make_async_copy(o_down, ddown, loc_sem.at[3])
    out_down.start()

    for copy in a1:
        copy.wait_recv()
    a2 = window(ha, None, CLS, a2_s, a2_r, False)
    for copy in a2:
        copy.start()

    def grads(which, n):
        def body(i, _):
            at = rows_of(CLS * which + CH * i, CH)
            h = ha[at, :].astype(F32)
            gu_o[at, 0:128] = (h * coef_b[at, :]).astype(BF16)
            gu_o[at, 128:256] = (h * coef_a[at, :]).astype(BF16)
            return 0

        lax.fori_loop(0, NK, body, 0)
        at = rows_of(CLS * which, CLS)
        copy = rcopy(gu_o.at[at], gu_s.at[at], sib_s.at[3 + n], sib_r.at[3 + n], sib)
        copy.start()
        return copy

    gu = [grads(cls, 0)]
    a2[2].wait_recv()
    gu.append(grads(near(-1), 1))
    a2[3].wait_recv()
    gu.append(grads(near(1), 2))
    a2[0].wait_recv()
    a2[1].wait_recv()
    gu.append(grads(near(2), 3))

    loc[1].wait()
    loc[2].wait()

    def input_part(buf):
        acc = jnp.zeros((ROWS, 128), F32)
        for j in range(J):
            w = jnp.concatenate(
                [wgv[:, 128 * j : 128 * j + 128], wuv[:, 128 * j : 128 * j + 128]], axis=1
            )
            acc = acc + lax.dot_general(
                buf[ROWS * j : ROWS * (j + 1), :], w, (((1,), (1,)), ((), ())),
                preferred_element_type=F32,
            )
        return acc

    part[c] = input_part(gu_o)
    for copy in gu:
        copy.wait_recv()
    part[1 - c] = input_part(gu_s)
    for i in range(NT):
        for p in range(2):
            rs_src[i, 12 * p : 12 * p + 12, :] = part[p, 12 * i : 12 * i + 12, :]
    rs = [
        rcopy(
            rs_src.at[lax.rem(t + i, NT)], rs_dst.at[t], rs_s.at[i - 1], rs_r.at[i - 1], tdev(i)
        )
        for i in (10, 5, 6, 7, 9, 11, 2, 8, 14, 13, 3, 1, 15, 4, 12)
    ]
    for copy in rs:
        copy.start()
    rs_dst[t] = rs_src[t]

    for j in range(J):
        both = jnp.concatenate(
            [gu_o[ROWS * j : ROWS * (j + 1), :], gu_s[ROWS * j : ROWS * (j + 1), :]], axis=0
        )
        val = jnp.dot(xot[...], both, preferred_element_type=F32).astype(BF16)
        o_gate[:, 128 * j : 128 * j + 128] = val[:, 0:128]
        o_up[:, 128 * j : 128 * j + 128] = val[:, 128:256]
    outs = [
        pltpu.make_async_copy(o_gate, dgate, loc_sem.at[4]),
        pltpu.make_async_copy(o_up, dup, loc_sem.at[5]),
    ]
    for copy in outs:
        copy.start()

    sends = xy + [wd_copy, og_copy] + sum(chains, []) + r1 + r2c + glo + a1 + [hid_copy] + a2 + gu
    for copy in sends:
        copy.wait_send()
    for copy in rs:
        copy.wait()
    total = rs_dst[0]
    for i in range(1, NT):
        total = total + rs_dst[i]
    fin[0] = total
    for p in range(2):
        for h in range(2):
            fin[1, 12 * h + 6 * p : 12 * h + 6 * p + 6, :] = fin[
                0, 12 * p + 6 * h : 12 * p + 6 * h + 6, :
            ]
    gin[...] = fin[1].astype(BF16)
    out_down.wait()
    for copy in outs:
        copy.wait()


def on_device(
    x_quant, x_scale, x_outlier, x_correction, g_quant, g_scale, g_outlier, g_correction,
    gate_pre, up_pre, w_gate, w_up, w_down,
):
    vmem = pl.BlockSpec(memory_space=pltpu.VMEM)
    smem = pl.BlockSpec(memory_space=pltpu.SMEM)
    anywhere = pl.BlockSpec(memory_space=pl.ANY)
    v, dma = pltpu.VMEM, pltpu.SemaphoreType.DMA
    return pl.pallas_call(
        kernel,
        name="ffn_backward",
        out_shape=(
            jax.ShapeDtypeStruct((24, 128), BF16),
            jax.ShapeDtypeStruct((128, 128 * J), BF16),
            jax.ShapeDtypeStruct((128, 128 * J), BF16),
            jax.ShapeDtypeStruct((128 * J, 128), BF16),
        ),
        in_specs=[smem] * 4 + [vmem] * 6 + [anywhere] * 3,
        out_specs=(vmem, anywhere, anywhere, anywhere),
        scratch_shapes=[
            v((NT, XY, 128), BF16),
            v((4, XY, 128), F32),
            v((4, ROWS, 128), F32),
            v((4, ROWS, 128), BF16),
            v((128, 2 * ROWS), BF16),
            v((ROWS, 256), BF16),
            v((2 * ROWS, 128), BF16),
            v((128 * J, 256), BF16),
            v((128, 128 * J), BF16),
            v((128, 128 * J), BF16),
            v((GCH, 128), F32),
            v((NZ * GCH, 128), BF16),
            v((8, GCH, 128), F32),
            v((J, 48, 128), F32),
            v((J, 48, 128), F32),
            v((FLAT, 128), F32),
            v((FLAT, 128), F32),
            v((FLAT, 128), BF16),
            v((FLAT, 128), BF16),
            v((FLAT, 128), F32),
            v((FLAT, 128), BF16),
            v((CLS, 128), BF16),
            v((CLS, 128), BF16),
            v((CLS, 128), BF16),
            v((CLS, 128), BF16),
            v((CLS, 128), F32),
            v((NK, CH, 128), BF16),
            v((FLAT, 128), BF16),
            v((FLAT, 256), BF16),
            v((FLAT, 256), BF16),
            v((2, ROWS, 128), F32),
            v((NT, 24, 128), F32),
            v((NT, 24, 128), F32),
            v((2, 24, 128), F32),
            v((128, 128 * J), BF16),
            v((128, 128 * J), BF16),
            v((128 * J, 128), BF16),
            dma((6,)),
            dma((7,)), dma((7,)),
            dma((NT - 1,)), dma((NT - 1,)),
            dma((NK - 1,)), dma((NK - 1,)),
            dma((4,)), dma((4,)),
            dma((4,)), dma((4,)),
            dma((NK - 1,)), dma((NK - 1,)),
            dma((NK - 1,)), dma((NK - 1,)),
            dma((4,)), dma((4,)),
            dma((NT - 1,)), dma((NT - 1,)),
        ],
        compiler_params=pltpu.CompilerParams(
            collective_id=0, has_side_effects=True, vmem_limit_bytes=48 * 1024 * 1024
        ),
        cost_estimate=pl.CostEstimate(
            flops=1_200_000_000, bytes_accessed=8_000_000, transcendentals=400_000
        ),
    )(
        x_scale, x_outlier, g_scale, g_outlier, x_quant, x_correction, g_quant, g_correction,
        gate_pre, up_pre, w_down, w_gate, w_up,
    )


def solution(mesh):
    both = P("tensor", "dp")
    return jax.shard_map(
        on_device,
        mesh=mesh,
        in_specs=(both,) * 8 + (P("dp", "tensor"),) * 4 + (both,),
        out_specs=(both, P("dp", "tensor"), P("dp", "tensor"), both),
        check_vma=False,
    )
```

time: 1100 us -> 139 us (0.13)
  waiting for transfers between devices: 1020 us -> 0 us
  Pallas kernels: 0 us -> 126 us
  blocking collectives: 37.4 us -> 0 us
  between operations: 17.5 us -> 3.27 us
    unnamed x8 -> x0, waiting for transfers between devices: 517 us -> none
    all_gather x4 -> x0, waiting for transfers between devices: 500 us -> none  [the longest x1 129 us: on_device(): lax.all_gather(up_pre, 'dp', axis=0, tiled=True).astype(jnp.float32)]
    pallas_call x0 -> x1, Pallas kernels: none -> 126 us  [on_device(): pl.pallas_call(kernel, name='ffn_backward', out_shape=(jax.ShapeDtypeStru...]
    all_gather x2 -> x0, blocking collectives: 37.4 us -> none  [the longest x1 19.3 us: on_device(): lax.all_gather(out_grad, 'tensor', axis=0, tiled=True)]
  transfers between devices with their start and end apart: 6 -> 0, of which waited for: 6 -> 0; matrix products, arithmetic and copies ran while one was open for 2% -> 0% of each run, Pallas kernels for 0% -> 0%
where the time goes in v1:
time: 139 us
  Pallas kernels  126 us (91%)
  local copies, waits for them, and re-layouts  9.44 us (7%)
  between operations  3.27 us (2%)
    pallas_call x1, Pallas kernels, on_device(): pl.pallas_call(kernel, name='ffn_backward', out_shape=(jax.ShapeDtypeStru...  126 us
    unnamed x22, local copies, waits for them, and re-layouts  9.44 us

profile of v1, /device:TPU:1, one launch (start us, length us, event | category | flops | bytes accessed | tf_op | source)
XLA Modules:
  0.0 138.9 jit_solution(2411249844635476577)
XLA Ops:
  0.6 0.0 copy-start.5
  3.2 0.0 copy-done.5
  3.2 0.0 copy-start
  3.3 1.0 copy-done
  4.3 0.0 copy-start.1
  4.3 1.0 copy-done.1
  5.3 0.0 copy-start.2
  5.3 1.0 copy-done.2
  6.3 0.0 copy-start.3
  6.3 0.7 copy-done.3
  7.0 0.0 copy-start.4
  7.0 0.7 copy-done.4
  7.8 0.0 copy-start.6
  7.8 0.7 copy-done.6
  8.5 0.0 copy-start.7
  8.5 0.7 copy-done.7
  9.1 0.0 copy-start.8
  9.1 0.7 copy-done.8
  9.8 126.2 %ffn_backward.1 = (bf16[24,128]{1,0:T(8,128)(2,1)S(1)}, bf16[128,1664]{1,0:T(8,128)(2,1)S(1)}, bf16[128,1664]{1,0:T(8,128)(2,1)S(1)}, bf16[1664,128]{1,0:T(8,128)(2,1)S(1)}) custom-call(f32[1,1]{1,0:T(1,128)S(6)} %copy.21.xs, s32[1,1]{1,0:T(1,128)S(6)} %copy.22.xo, f32[1,1]{1,0:T(1,128)S(6)} %copy.23.gs, s32[1,1]{1,0:T(1,128)S(6)} %copy.24.go, ...), custom_call_target="tpu_custom_call" | custom-call | flops 1200000000 | bytes 8000000 | tf_op jit(solution)/shard_map/ffn_backward/pallas_call | solution.py:365
  136.0 0.6 copy.25
  136.6 0.8 copy.26
  137.4 0.8 copy.27
  138.2 0.8 copy.28
Async XLA Ops:
  0.6 2.6 %copy-start.5 = (bf16[24,128]{1,0:T(8,128)(2,1)S(1)}, bf16[24,128]{1,0:T(8,128)(2,1)}, u32[]{:S(2)}) copy-start(bf16[24,128]{1,0:T(8,128)(2,1)} %xq.1) | copy-start | bytes 18436
  3.2 1.0 copy-start
  4.3 1.0 copy-start.1
  5.3 1.0 copy-start.2
  6.3 0.7 copy-start.3
  7.0 0.7 copy-start.4
  7.8 0.7 copy-start.6
  8.5 0.7 copy-start.7
  9.1 0.7 copy-start.8

commit v2 on v1

v2 whole, which is shorter than its diff:
```python
import jax
import jax.numpy as jnp
from jax import lax
from jax.experimental import pallas as pl
from jax.experimental.pallas import tpu as pltpu
from jax.sharding import PartitionSpec as P

MESH = pl.DeviceIdType.MESH
F32, BF16 = jnp.float32, jnp.bfloat16

NZ, STRIDE = 32, 4
NK = NZ // STRIDE
NT = 16
J = 13
ROWS = 192
CH = 80
FLAT = NZ * CH
CLS = NK * CH
GCH = 2 * CH
GCLS = NK * GCH
XY = 48


def rows_of(start, size, align=16):
    return pl.ds(pl.multiple_of(start, align), size)


def kernel(
    xs_in, xo_in, gs_in, go_in, xq_in, xc_in, gq_in, gc_in, gate_in, up_in, wd, wg, wu,
    gin, dgate, dup, ddown,
    xs, xo, gs, go, xq, xc, gq, gc, gate, up,
    xyb, tmp48, u4, xg, xot, og2, ogall, wd2, wgv, wuv,
    gpack, gbuf, tt, tg, tu, coef_a, coef_b, hid_o, hid_s,
    hf, hp, r1b, r2s, r2r, ha,
    gu_o, gu_s, part, rs_src, rs_dst, fin, o_in, o_gate, o_up, o_down,
    in_sem, loc_sem, sib_s, sib_r, xy_s, xy_r, gch_s, gch_r, glo_s, glo_r,
    r1_s, r1_r, r2_s, r2_r, a1_s, a1_r, a2_s, a2_r, gu_ss, gu_rs, rs_s, rs_r,
):
    dp, t = lax.axis_index("dp"), lax.axis_index("tensor")
    z, c = dp // 2, lax.rem(dp, 2)
    k0, cls = z // STRIDE, lax.rem(z, STRIDE)

    def zdev(d):
        return (lax.rem(dp + 2 * d + 2 * NZ, 2 * NZ), t)

    def tdev(i):
        return (dp, lax.rem(t + i, NT))

    sib = (dp + 1 - 2 * c, t)

    def rcopy(src, dst, ss, rs, dev):
        return pltpu.make_async_remote_copy(
            src_ref=src, dst_ref=dst, send_sem=ss, recv_sem=rs, device_id=dev, device_id_type=MESH
        )

    barrier = pltpu.get_barrier_semaphore()
    peers = [zdev(d) for d in (1, -1, 2, -2, STRIDE, -STRIDE)]
    peers += [sib] + [tdev(i) for i in range(1, NT)]
    for peer in peers:
        pl.semaphore_signal(barrier, inc=1, device_id=peer, device_id_type=MESH)

    loc = [
        pltpu.make_async_copy(wd, wd2.at[:, pl.ds(0, 128)], loc_sem.at[0]),
        pltpu.make_async_copy(wg, wgv, loc_sem.at[1]),
        pltpu.make_async_copy(wu, wuv, loc_sem.at[2]),
    ]
    small = [
        pltpu.make_async_copy(src, dst, in_sem.at[n])
        for n, (src, dst) in enumerate(
            (
                (xq_in, xq), (xc_in, xc), (gq_in, gq), (gc_in, gc), (xs_in, xs), (xo_in, xo),
                (gs_in, gs), (go_in, go), (gate_in, gate), (up_in, up),
            )
        )
    ]
    for copy in small + loc:
        copy.start()
    for copy in small:
        copy.wait()

    fin[0] = xs[0, 0] * xq[...].astype(F32) + xo[0, 0].astype(F32) * xc[...].astype(F32)
    fin[1] = gs[0, 0] * gq[...].astype(F32) + go[0, 0].astype(F32) * gc[...].astype(F32)
    for a in range(2):
        for p in range(2):
            for h in range(2):
                tmp48[0, 24 * a + 12 * p + 6 * h : 24 * a + 12 * p + 6 * h + 6, :] = fin[
                    a, 12 * h + 6 * p : 12 * h + 6 * p + 6, :
                ]
    xyb[t] = tmp48[0].astype(BF16)

    def near(d):
        return lax.rem(cls + d + STRIDE, STRIDE)

    def k_of(d):
        return lax.rem(z + d + NZ, NZ) // STRIDE

    class Gather:
        which = (0, -1, -2, -3, -4, 1, 2, 3)
        towards = (1, -1, -2)

        def __init__(self, buf, ch, chain_s, chain_r, local_s, local_r):
            self.ch = ch

            def slot(n):
                return buf.at[self.rows(0, n)]

            def link(n, at, d):
                return rcopy(slot(n), slot(n), chain_s.at[at], chain_r.at[at], zdev(d))

            self.right = [link(n, n, STRIDE) for n in range(4)]
            self.left = [link((0, 5, 6)[n], 4 + n, -STRIDE) for n in range(3)]
            self.local = [
                [
                    rcopy(slot(n), slot(n), local_s.at[m, n], local_r.at[m, n], zdev(d))
                    for m, d in enumerate(self.towards)
                ]
                for n in range(NK)
            ]
            self.all = self.right + self.left + sum(self.local, [])

        def rows(self, d, n):
            k = lax.rem(k_of(d) + self.which[n] + NK, NK)
            return rows_of(NK * self.ch * near(d) + self.ch * k, self.ch)

        def begin(self):
            self.right[0].start()
            self.left[0].start()
            self.spread(0)

        def spread(self, n):
            for copy in self.local[n]:
                copy.start()

        def step(self, i):
            self.right[i - 1].wait_recv()
            if i < 4:
                self.right[i].start()
                self.left[i - 1].wait_recv()
            if i < 3:
                self.left[i].start()
            self.spread(i)
            if i < 4:
                self.spread(4 + i)

        def arrive(self, n):
            for copy in self.local[n]:
                copy.wait_recv()

    gpack[...] = jnp.zeros_like(gpack)
    gate_val, up_val = gate[...].astype(F32), up[...].astype(F32)
    for j in range(J):
        gpack[6 * j : 6 * j + 6, :] = gate_val[:, 128 * j : 128 * j + 128]
        gpack[CH + 6 * j : CH + 6 * j + 6, :] = up_val[:, 128 * j : 128 * j + 128]

    saved = Gather(gbuf, GCH, gch_s, gch_r, glo_s, glo_r)
    gbuf[saved.rows(0, 0), :] = gpack[...].astype(BF16)
    pl.semaphore_wait(barrier, len(peers))

    xy = [
        rcopy(xyb.at[t], xyb.at[t], xy_s.at[i - 1], xy_r.at[i - 1], tdev(i))
        for i in (10, 5, 6, 7, 9, 11, 2, 8, 14, 13, 3, 1, 15, 4, 12)
    ]
    for copy in xy:
        copy.start()
    wd_copy = rcopy(wd, wd2.at[:, pl.ds(128, 128)], sib_s.at[0], sib_r.at[0], sib)
    wd_copy.start()

    saved.begin()

    for copy in xy:
        copy.wait_recv()
    for i in range(NT):
        tmp48[i % 4] = xyb[i].astype(F32)
        for a in range(4):
            u4[a, 12 * i : 12 * i + 12, :] = tmp48[i % 4, 12 * a : 12 * a + 12, :]
    for a in range(4):
        xg[a] = u4[a].astype(BF16)
    og_copy = rcopy(xg.at[3 - c], og2.at[:, pl.ds(128, 128)], sib_s.at[1], sib_r.at[1], sib)
    og_copy.start()
    saved.step(1)
    og2[:, 0:128] = xg[2 + c]
    ogall[0:ROWS, :] = xg[2 + c]
    ogall[ROWS : 2 * ROWS, :] = xg[3 - c]
    tx = jnp.concatenate([u4[c], u4[1 - c]], axis=0)
    xot[...] = jnp.transpose(tx).astype(BF16)
    loc[0].wait()
    wd_copy.wait_recv()
    og_copy.wait_recv()

    hp[J * ROWS : FLAT, :] = jnp.zeros((FLAT - J * ROWS, 128), BF16)
    hf[J * ROWS : FLAT, :] = jnp.zeros((FLAT - J * ROWS, 128), F32)
    og_val = og2[...]
    for j in range(J):
        val = lax.dot_general(
            og_val, wd2[128 * j : 128 * j + 128, :], (((1,), (1,)), ((), ())),
            preferred_element_type=F32,
        )
        hf[ROWS * j : ROWS * (j + 1), :] = val
        hp[ROWS * j : ROWS * (j + 1), :] = val.astype(BF16)

    r1 = {}
    for off in (4, 5, 3, 6, 2, 7, 1, 0):
        for n, d in enumerate((1, -1, 2)):
            base = CLS * near(d) + CH * lax.rem(k_of(d) + off, NK)
            r1[off, n] = rcopy(
                hp.at[rows_of(base, CH)], r1b.at[n, off], r1_s.at[n, off], r1_r.at[n, off], zdev(d)
            )
            r1[off, n].start()

    def window_sum(off):
        total = hf[rows_of(CLS * cls + CH * lax.rem(k0 + off, NK), CH), :]
        for n in range(3):
            r1[off, n].wait_recv()
            total = total + r1b[n, off].astype(F32)
        return total

    saved.step(2)
    r2 = {}
    for i in range(1, 5):
        for w, off, d in ((0, 5 - i, STRIDE), (1, 4 + i, -STRIDE)):
            if w == 1 and i == 4:
                continue
            total = window_sum(off)
            if i > 1:
                r2[w, i - 1].wait_recv()
                total = total + r2r[w, i - 2].astype(F32)
            r2s[w, i - 1] = total.astype(BF16)
            r2[w, i] = rcopy(
                r2s.at[w, i - 1], r2r.at[w, i - 1], r2_s.at[w, i - 1], r2_r.at[w, i - 1], zdev(d)
            )
            r2[w, i].start()
        if i < 3:
            saved.step(2 + i)
    total = window_sum(0)
    r2[1, 3].wait_recv()
    total = total + r2r[1, 2].astype(F32)
    r2[0, 4].wait_recv()
    total = total + r2r[0, 3].astype(F32)
    back = Gather(ha, CH, a1_s, a1_r, a2_s, a2_r)
    ha[back.rows(0, 0), :] = total.astype(BF16)
    back.begin()

    for n in range(NK):
        saved.arrive(n)
    coef_a[J * ROWS : FLAT, :] = jnp.zeros((FLAT - J * ROWS, 128), F32)
    coef_b[J * ROWS : FLAT, :] = jnp.zeros((FLAT - J * ROWS, 128), F32)

    def factors(m, _):
        for q in range(8):
            start = GCLS * (q % STRIDE) + GCH * (q // STRIDE) + 2 * GCH * m
            tt[q] = gbuf[rows_of(start, GCH), :].astype(F32)
            for j in range(J):
                tg[j, 6 * q : 6 * q + 6, :] = tt[q, 6 * j : 6 * j + 6, :]
                tu[j, 6 * q : 6 * q + 6, :] = tt[q, CH + 6 * j : CH + 6 * j + 6, :]

        def tile(j, _):
            g, u = tg[j], tu[j]
            s = 1.0 / (1.0 + jnp.exp(-g))
            silu = g * s
            at = rows_of(ROWS * j + 48 * m, 48)
            hid_o[at, :] = (silu * u).astype(BF16)
            coef_a[at, :] = silu
            coef_b[at, :] = u * s * (1.0 + g * (1.0 - s))
            return 0

        lax.fori_loop(0, J, tile, 0)
        return 0

    lax.fori_loop(0, 4, factors, 0)
    hid_copy = rcopy(hid_o, hid_s, sib_s.at[2], sib_r.at[2], sib)
    hid_copy.start()
    back.step(1)
    hid_copy.wait_recv()

    def down(j, _):
        at = rows_of(ROWS * j, ROWS)
        both = jnp.concatenate([hid_o[at, :], hid_s[at, :]], axis=0)
        val = lax.dot_general(
            both, ogall[...], (((0,), (0,)), ((), ())), preferred_element_type=F32
        )
        o_down[rows_of(128 * j, 128), :] = val.astype(BF16)
        return 0

    lax.fori_loop(0, J, down, 0)

    outs = [pltpu.make_async_copy(o_down, ddown, loc_sem.at[3])]
    outs[0].start()

    gu = []

    def grads(d, n):
        at = back.rows(d, n)
        h = ha[at, :].astype(F32)
        gu_o[at, 0:128] = (h * coef_b[at, :]).astype(BF16)
        gu_o[at, 128:256] = (h * coef_a[at, :]).astype(BF16)
        m = len(gu)
        gu.append(rcopy(gu_o.at[at], gu_s.at[at], gu_ss.at[m], gu_rs.at[m], sib))
        gu[m].start()

    def arrived(n):
        for m, d in enumerate(back.towards):
            back.local[n][m].wait_recv()
            grads(-d, n)

    grads(0, 0)
    for n in (1, 5):
        grads(0, n)
    arrived(0)
    back.step(2)
    grads(0, 2)
    grads(0, 6)
    arrived(1)
    arrived(5)
    back.step(3)
    grads(0, 3)
    grads(0, 7)
    arrived(2)
    arrived(6)
    back.step(4)
    grads(0, 4)
    arrived(3)
    arrived(7)
    arrived(4)

    loc[1].wait()
    loc[2].wait()

    def input_part(buf):
        acc = jnp.zeros((ROWS, 128), F32)
        for j in range(J):
            w = jnp.concatenate(
                [wgv[:, 128 * j : 128 * j + 128], wuv[:, 128 * j : 128 * j + 128]], axis=1
            )
            acc = acc + lax.dot_general(
                buf[ROWS * j : ROWS * (j + 1), :], w, (((1,), (1,)), ((), ())),
                preferred_element_type=F32,
            )
        return acc

    part[c] = input_part(gu_o)
    for copy in gu:
        copy.wait_recv()
    part[1 - c] = input_part(gu_s)
    for i in range(NT):
        for p in range(2):
            rs_src[i, 12 * p : 12 * p + 12, :] = part[p, 12 * i : 12 * i + 12, :]
    rs = [
        rcopy(
            rs_src.at[lax.rem(t + i, NT)], rs_dst.at[t], rs_s.at[i - 1], rs_r.at[i - 1], tdev(i)
        )
        for i in (10, 5, 6, 7, 9, 11, 2, 8, 14, 13, 3, 1, 15, 4, 12)
    ]
    for copy in rs:
        copy.start()
    rs_dst[t] = rs_src[t]

    for j in range(J):
        both = jnp.concatenate(
            [gu_o[ROWS * j : ROWS * (j + 1), :], gu_s[ROWS * j : ROWS * (j + 1), :]], axis=0
        )
        val = jnp.dot(xot[...], both, preferred_element_type=F32).astype(BF16)
        o_gate[:, 128 * j : 128 * j + 128] = val[:, 0:128]
        o_up[:, 128 * j : 128 * j + 128] = val[:, 128:256]
    outs.append(pltpu.make_async_copy(o_gate, dgate, loc_sem.at[4]))
    outs.append(pltpu.make_async_copy(o_up, dup, loc_sem.at[5]))
    outs[1].start()
    outs[2].start()

    sends = xy + [wd_copy, og_copy, hid_copy] + saved.all + back.all + gu
    sends += list(r1.values()) + list(r2.values())
    for copy in sends:
        copy.wait_send()
    for copy in rs:
        copy.wait()
    total = rs_dst[0]
    for i in range(1, NT):
        total = total + rs_dst[i]
    fin[0] = total
    for p in range(2):
        for h in range(2):
            fin[1, 12 * h + 6 * p : 12 * h + 6 * p + 6, :] = fin[
                0, 12 * p + 6 * h : 12 * p + 6 * h + 6, :
            ]
    o_in[...] = fin[1].astype(BF16)
    outs.append(pltpu.make_async_copy(o_in, gin, loc_sem.at[6]))
    outs[3].start()
    for copy in outs:
        copy.wait()


def on_device(
    x_quant, x_scale, x_outlier, x_correction, g_quant, g_scale, g_outlier, g_correction,
    gate_pre, up_pre, w_gate, w_up, w_down,
):
    hbm = pl.BlockSpec(memory_space=pltpu.HBM)
    v, m, dma = pltpu.VMEM, pltpu.SMEM, pltpu.SemaphoreType.DMA
    return pl.pallas_call(
        kernel,
        name="ffn_backward",
        out_shape=(
            jax.ShapeDtypeStruct((24, 128), BF16),
            jax.ShapeDtypeStruct((128, 128 * J), BF16),
            jax.ShapeDtypeStruct((128, 128 * J), BF16),
            jax.ShapeDtypeStruct((128 * J, 128), BF16),
        ),
        in_specs=[hbm] * 13,
        out_specs=(hbm,) * 4,
        scratch_shapes=[
            m((1, 1), F32), m((1, 1), jnp.int32), m((1, 1), F32), m((1, 1), jnp.int32),
            v((24, 128), BF16), v((24, 128), BF16), v((24, 128), BF16), v((24, 128), BF16),
            v((6, 128 * J), BF16), v((6, 128 * J), BF16),
            v((NT, XY, 128), BF16),
            v((4, XY, 128), F32),
            v((4, ROWS, 128), F32),
            v((4, ROWS, 128), BF16),
            v((128, 2 * ROWS), BF16),
            v((ROWS, 256), BF16),
            v((2 * ROWS, 128), BF16),
            v((128 * J, 256), BF16),
            v((128, 128 * J), BF16),
            v((128, 128 * J), BF16),
            v((GCH, 128), F32),
            v((NZ * GCH, 128), BF16),
            v((8, GCH, 128), F32),
            v((J, 48, 128), F32),
            v((J, 48, 128), F32),
            v((FLAT, 128), F32),
            v((FLAT, 128), F32),
            v((FLAT, 128), BF16),
            v((FLAT, 128), BF16),
            v((FLAT, 128), F32),
            v((FLAT, 128), BF16),
            v((3, NK, CH, 128), BF16),
            v((2, 4, CH, 128), BF16),
            v((2, 4, CH, 128), BF16),
            v((FLAT, 128), BF16),
            v((FLAT, 256), BF16),
            v((FLAT, 256), BF16),
            v((2, ROWS, 128), F32),
            v((NT, 24, 128), F32),
            v((NT, 24, 128), F32),
            v((2, 24, 128), F32),
            v((24, 128), BF16),
            v((128, 128 * J), BF16),
            v((128, 128 * J), BF16),
            v((128 * J, 128), BF16),
            dma((10,)), dma((7,)),
            dma((3,)), dma((3,)),
            dma((NT - 1,)), dma((NT - 1,)),
            dma((NK - 1,)), dma((NK - 1,)),
            dma((3, NK)), dma((3, NK)),
            dma((3, NK)), dma((3, NK)),
            dma((2, 4)), dma((2, 4)),
            dma((NK - 1,)), dma((NK - 1,)),
            dma((3, NK)), dma((3, NK)),
            dma((NZ,)), dma((NZ,)),
            dma((NT - 1,)), dma((NT - 1,)),
        ],
        compiler_params=pltpu.CompilerParams(
            collective_id=0, has_side_effects=True, vmem_limit_bytes=63 * 1024 * 1024
        ),
        cost_estimate=pl.CostEstimate(
            flops=1_200_000_000, bytes_accessed=8_000_000, transcendentals=400_000
        ),
    )(
        x_scale, x_outlier, g_scale, g_outlier, x_quant, x_correction, g_quant, g_correction,
        gate_pre, up_pre, w_down, w_gate, w_up,
    )


def solution(mesh):
    both = P("tensor", "dp")
    return jax.shard_map(
        on_device,
        mesh=mesh,
        in_specs=(both,) * 8 + (P("dp", "tensor"),) * 4 + (both,),
        out_specs=(both, P("dp", "tensor"), P("dp", "tensor"), both),
        check_vma=False,
    )
```

time: 139 us -> 115 us (0.83)
  Pallas kernels: 126 us -> 106 us
  local copies, waits for them, and re-layouts: 9.44 us -> 5.05 us
    pallas_call x1, Pallas kernels: 126 us -> 106 us  [on_device(): pl.pallas_call(kernel, name='ffn_backward', out_shape=(jax.ShapeDtypeStru...]
    unnamed x22 -> x10, local copies, waits for them, and re-layouts: 9.44 us -> 5.05 us
where the time goes in v2:
time: 115 us
  Pallas kernels  106 us (92%)
  local copies, waits for them, and re-layouts  5.05 us (4%)
  between operations  3.24 us (3%)
    pallas_call x1, Pallas kernels, on_device(): pl.pallas_call(kernel, name='ffn_backward', out_shape=(jax.ShapeDtypeStru...  106 us
    unnamed x10, local copies, waits for them, and re-layouts  5.05 us

profile of v2, /device:TPU:1, one launch (start us, length us, event | category | flops | bytes accessed | tf_op | source)
XLA Modules:
  0.0 114.8 jit_solution(15292476517222479247)
XLA Ops:
  3.2 106.5 %ffn_backward.1 = (bf16[24,128]{1,0:T(8,128)(2,1)}, bf16[128,1664]{1,0:T(8,128)(2,1)}, bf16[128,1664]{1,0:T(8,128)(2,1)}, bf16[1664,128]{1,0:T(8,128)(2,1)}) custom-call(f32[1,1]{1,0:T(1,128)S(6)} %copy.21.xs_in, s32[1,1]{1,0:T(1,128)S(6)} %copy.22.xo_in, f32[1,1]{1,0:T(1,128)S(6)} %copy.23.gs_in, s32[1,1]{1,0:T(1,128)S(6)} %copy.24.go_in, ...), custom_call_target="tpu_custom_call" | custom-call | flops 1200000000 | bytes 8000000 | tf_op jit(solution)/shard_map/ffn_backward/pallas_call | solution.py:397
  109.7 0.0 copy-start.2
  109.7 0.7 copy-done.2
  110.4 0.6 copy.25
  111.0 0.0 copy-start.1
  111.0 1.8 %copy.26 = bf16[128,1664]{1,0:T(8,128)(2,1)} copy(bf16[128,1664]{1,0:T(8,128)(2,1)} %get-tuple-element.9) | data formatting | bytes 851968
  112.8 0.0 copy-done.1
  112.8 0.0 copy-start
  112.8 0.8 copy.27
  113.6 0.4 copy-done
  114.0 0.8 copy.28
Async XLA Ops:
  109.7 0.7 copy-start.2
  111.0 1.9 %copy-start.1 = (bf16[128,1664]{1,0:T(8,128)(2,1)S(1)}, bf16[128,1664]{1,0:T(8,128)(2,1)}, u32[]{:S(2)}) copy-start(bf16[128,1664]{1,0:T(8,128)(2,1)} %get-tuple-element.10) | copy-start | bytes 1277956
  112.8 1.2 %copy-start = (bf16[1664,128]{1,0:T(8,128)(2,1)S(1)}, bf16[1664,128]{1,0:T(8,128)(2,1)}, u32[]{:S(2)}) copy-start(bf16[1664,128]{1,0:T(8,128)(2,1)} %get-tuple-element.11) | copy-start | bytes 1277956

commit v3 on v2

--- a/solution.py
+++ b/solution.py
@@ -17,7 +17,6 @@
 FLAT = NZ * CH
 CLS = NK * CH
 GCH = 2 * CH
-GCLS = NK * GCH
 XY = 48
 
 
@@ -95,11 +94,11 @@
         return lax.rem(z + d + NZ, NZ) // STRIDE
 
     class Gather:
-        which = (0, -1, -2, -3, -4, 1, 2, 3)
-        towards = (1, -1, -2)
-
-        def __init__(self, buf, ch, chain_s, chain_r, local_s, local_r):
-            self.ch = ch
+        def __init__(self, buf, ch, stride, towards, chain_s, chain_r, local_s, local_r):
+            self.ch, self.stride, self.towards = ch, stride, towards
+            self.nk = nk = NZ // stride
+            self.half = half = nk // 2
+            self.which = tuple(range(0, -half - 1, -1)) + tuple(range(1, half))
 
             def slot(n):
                 return buf.at[self.rows(0, n)]
@@ -107,20 +106,31 @@
             def link(n, at, d):
                 return rcopy(slot(n), slot(n), chain_s.at[at], chain_r.at[at], zdev(d))
 
-            self.right = [link(n, n, STRIDE) for n in range(4)]
-            self.left = [link((0, 5, 6)[n], 4 + n, -STRIDE) for n in range(3)]
-            self.local = [
-                [
-                    rcopy(slot(n), slot(n), local_s.at[m, n], local_r.at[m, n], zdev(d))
-                    for m, d in enumerate(self.towards)
-                ]
-                for n in range(NK)
-            ]
+            self.right = [link(n, n, stride) for n in range(half)]
+            self.left = [link(half + n if n else 0, half + n, -stride) for n in range(half - 1)]
+            self.local = []
+            for n in range(nk):
+                if towards:
+                    self.local.append(
+                        [
+                            rcopy(slot(n), slot(n), local_s.at[m, n], local_r.at[m, n], zdev(d))
+                            for m, d in enumerate(towards)
+                        ]
+                    )
+                else:
+                    at = self.index(0, n)
+                    to = (lax.rem(dp + 2 - 4 * lax.rem(at, 2) + 2 * NZ, 2 * NZ), t)
+                    self.local.append(
+                        [rcopy(slot(n), slot(n), local_s.at[n], local_r.at[at], to)]
+                    )
             self.all = self.right + self.left + sum(self.local, [])
 
+        def index(self, d, n):
+            return lax.rem(lax.rem(z + d + NZ, NZ) // self.stride + self.which[n] + self.nk, self.nk)
+
         def rows(self, d, n):
-            k = lax.rem(k_of(d) + self.which[n] + NK, NK)
-            return rows_of(NK * self.ch * near(d) + self.ch * k, self.ch)
+            cls_at = lax.rem(lax.rem(z, self.stride) + d + self.stride, self.stride)
+            return rows_of(self.ch * (self.nk * cls_at + self.index(d, n)), self.ch)
 
         def begin(self):
             self.right[0].start()
@@ -132,15 +142,16 @@
                 copy.start()
 
         def step(self, i):
+            half = self.half
             self.right[i - 1].wait_recv()
-            if i < 4:
+            if i < half:
                 self.right[i].start()
                 self.left[i - 1].wait_recv()
-            if i < 3:
+            if i < half - 1:
                 self.left[i].start()
             self.spread(i)
-            if i < 4:
-                self.spread(4 + i)
+            if i < half:
+                self.spread(half + i)
 
         def arrive(self, n):
             for copy in self.local[n]:
@@ -152,7 +163,7 @@
         gpack[6 * j : 6 * j + 6, :] = gate_val[:, 128 * j : 128 * j + 128]
         gpack[CH + 6 * j : CH + 6 * j + 6, :] = up_val[:, 128 * j : 128 * j + 128]
 
-    saved = Gather(gbuf, GCH, gch_s, gch_r, glo_s, glo_r)
+    saved = Gather(gbuf, GCH, 2, (), gch_s, gch_r, glo_s, glo_r)
     gbuf[saved.rows(0, 0), :] = gpack[...].astype(BF16)
     pl.semaphore_wait(barrier, len(peers))
 
@@ -167,6 +178,7 @@
 
     saved.begin()
 
+    saved.step(1)
     for copy in xy:
         copy.wait_recv()
     for i in range(NT):
@@ -177,7 +189,6 @@
         xg[a] = u4[a].astype(BF16)
     og_copy = rcopy(xg.at[3 - c], og2.at[:, pl.ds(128, 128)], sib_s.at[1], sib_r.at[1], sib)
     og_copy.start()
-    saved.step(1)
     og2[:, 0:128] = xg[2 + c]
     ogall[0:ROWS, :] = xg[2 + c]
     ogall[ROWS : 2 * ROWS, :] = xg[3 - c]
@@ -186,6 +197,7 @@
     loc[0].wait()
     wd_copy.wait_recv()
     og_copy.wait_recv()
+    saved.step(2)
 
     hp[J * ROWS : FLAT, :] = jnp.zeros((FLAT - J * ROWS, 128), BF16)
     hf[J * ROWS : FLAT, :] = jnp.zeros((FLAT - J * ROWS, 128), F32)
@@ -214,7 +226,7 @@
             total = total + r1b[n, off].astype(F32)
         return total
 
-    saved.step(2)
+    saved.step(3)
     r2 = {}
     for i in range(1, 5):
         for w, off, d in ((0, 5 - i, STRIDE), (1, 4 + i, -STRIDE)):
@@ -229,25 +241,26 @@
                 r2s.at[w, i - 1], r2r.at[w, i - 1], r2_s.at[w, i - 1], r2_r.at[w, i - 1], zdev(d)
             )
             r2[w, i].start()
-        if i < 3:
-            saved.step(2 + i)
+        saved.step(3 + i)
     total = window_sum(0)
     r2[1, 3].wait_recv()
     total = total + r2r[1, 2].astype(F32)
     r2[0, 4].wait_recv()
     total = total + r2r[0, 3].astype(F32)
-    back = Gather(ha, CH, a1_s, a1_r, a2_s, a2_r)
+    back = Gather(ha, CH, STRIDE, (1, -1, -2), a1_s, a1_r, a2_s, a2_r)
     ha[back.rows(0, 0), :] = total.astype(BF16)
     back.begin()
-
-    for n in range(NK):
+    saved.step(8)
+
+    back.step(1)
+    for n in range(NZ // 2):
         saved.arrive(n)
     coef_a[J * ROWS : FLAT, :] = jnp.zeros((FLAT - J * ROWS, 128), F32)
     coef_b[J * ROWS : FLAT, :] = jnp.zeros((FLAT - J * ROWS, 128), F32)
 
     def factors(m, _):
         for q in range(8):
-            start = GCLS * (q % STRIDE) + GCH * (q // STRIDE) + 2 * GCH * m
+            start = GCH * (NZ // 2 * (q % 2) + q // 2 + 4 * m)
             tt[q] = gbuf[rows_of(start, GCH), :].astype(F32)
             for j in range(J):
                 tg[j, 6 * q : 6 * q + 6, :] = tt[q, 6 * j : 6 * j + 6, :]
@@ -269,7 +282,27 @@
     lax.fori_loop(0, 4, factors, 0)
     hid_copy = rcopy(hid_o, hid_s, sib_s.at[2], sib_r.at[2], sib)
     hid_copy.start()
-    back.step(1)
+    gu = []
+
+    def grads(d, n):
+        at = back.rows(d, n)
+        h = ha[at, :].astype(F32)
+        gu_o[at, 0:128] = (h * coef_b[at, :]).astype(BF16)
+        gu_o[at, 128:256] = (h * coef_a[at, :]).astype(BF16)
+        m = len(gu)
+        gu.append(rcopy(gu_o.at[at], gu_s.at[at], gu_ss.at[m], gu_rs.at[m], sib))
+        gu[m].start()
+
+    def arrived(n):
+        for m, d in enumerate(back.towards):
+            back.local[n][m].wait_recv()
+            grads(-d, n)
+
+    grads(0, 0)
+    for n in (1, 5):
+        grads(0, n)
+    arrived(0)
+    back.step(2)
     hid_copy.wait_recv()
 
     def down(j, _):
@@ -286,27 +319,6 @@
     outs = [pltpu.make_async_copy(o_down, ddown, loc_sem.at[3])]
     outs[0].start()
 
-    gu = []
-
-    def grads(d, n):
-        at = back.rows(d, n)
-        h = ha[at, :].astype(F32)
-        gu_o[at, 0:128] = (h * coef_b[at, :]).astype(BF16)
-        gu_o[at, 128:256] = (h * coef_a[at, :]).astype(BF16)
-        m = len(gu)
-        gu.append(rcopy(gu_o.at[at], gu_s.at[at], gu_ss.at[m], gu_rs.at[m], sib))
-        gu[m].start()
-
-    def arrived(n):
-        for m, d in enumerate(back.towards):
-            back.local[n][m].wait_recv()
-            grads(-d, n)
-
-    grads(0, 0)
-    for n in (1, 5):
-        grads(0, n)
-    arrived(0)
-    back.step(2)
     grads(0, 2)
     grads(0, 6)
     arrived(1)
@@ -388,13 +400,37 @@
         copy.wait()
 
 
+def deliver_kernel(a, b, c, d, a_out, b_out, c_out, d_out, sem):
+    copies = [
+        pltpu.make_async_copy(src, dst, sem.at[n])
+        for n, (src, dst) in enumerate(((b, b_out), (c, c_out), (d, d_out), (a, a_out)))
+    ]
+    for copy in copies:
+        copy.start()
+    for copy in copies:
+        copy.wait()
+
+
+def deliver(*results):
+    hbm = pl.BlockSpec(memory_space=pltpu.HBM)
+    return pl.pallas_call(
+        deliver_kernel,
+        name="deliver",
+        out_shape=tuple(jax.ShapeDtypeStruct(r.shape, r.dtype) for r in results),
+        in_specs=[hbm] * 4,
+        out_specs=(hbm,) * 4,
+        scratch_shapes=[pltpu.SemaphoreType.DMA((4,))],
+        compiler_params=pltpu.CompilerParams(vmem_limit_bytes=63 * 1024 * 1024),
+    )(*results)
+
+
 def on_device(
     x_quant, x_scale, x_outlier, x_correction, g_quant, g_scale, g_outlier, g_correction,
     gate_pre, up_pre, w_gate, w_up, w_down,
 ):
     hbm = pl.BlockSpec(memory_space=pltpu.HBM)
     v, m, dma = pltpu.VMEM, pltpu.SMEM, pltpu.SemaphoreType.DMA
-    return pl.pallas_call(
+    results = pl.pallas_call(
         kernel,
         name="ffn_backward",
         out_shape=(
@@ -447,8 +483,8 @@
             dma((10,)), dma((7,)),
             dma((3,)), dma((3,)),
             dma((NT - 1,)), dma((NT - 1,)),
-            dma((NK - 1,)), dma((NK - 1,)),
-            dma((3, NK)), dma((3, NK)),
+            dma((NZ // 2 - 1,)), dma((NZ // 2 - 1,)),
+            dma((NZ // 2,)), dma((NZ // 2,)),
             dma((3, NK)), dma((3, NK)),
             dma((2, 4)), dma((2, 4)),
             dma((NK - 1,)), dma((NK - 1,)),
@@ -466,6 +502,7 @@
         x_scale, x_outlier, g_scale, g_outlier, x_quant, x_correction, g_quant, g_correction,
         gate_pre, up_pre, w_down, w_gate, w_up,
     )
+    return deliver(*results)
 
 
 def solution(mesh):

time: 115 us -> 146 us (1.27)
  Pallas kernels: 106 us -> 143 us
  local copies, waits for them, and re-layouts: 5.05 us -> 0 us
    pallas_call x0 -> x1, Pallas kernels: none -> 40 us  [deliver(): pl.pallas_call(deliver_kernel, name='deliver', out_shape=tuple((jax.Shape...]
    unnamed x10 -> x0, local copies, waits for them, and re-layouts: 5.05 us -> none
    pallas_call x1, Pallas kernels: 106 us -> 103 us  [on_device(): pl.pallas_call(kernel, name='ffn_backward', out_shape=(jax.ShapeDtypeStru...]
where the time goes in v3:
time: 146 us
  Pallas kernels  143 us (98%)
  between operations  3.22 us (2%)
    pallas_call x1, Pallas kernels, on_device(): pl.pallas_call(kernel, name='ffn_backward', out_shape=(jax.ShapeDtypeStru...  103 us
    pallas_call x1, Pallas kernels, deliver(): pl.pallas_call(deliver_kernel, name='deliver', out_shape=tuple((jax.Shape...  40 us

profile of v3, /device:TPU:1, one launch (start us, length us, event | category | flops | bytes accessed | tf_op | source)
XLA Modules:
  0.0 145.9 jit_solution(4727107179123027737)
XLA Ops:
  3.2 102.7 %ffn_backward.1 = (bf16[24,128]{1,0:T(8,128)(2,1)}, bf16[128,1664]{1,0:T(8,128)(2,1)}, bf16[128,1664]{1,0:T(8,128)(2,1)}, bf16[1664,128]{1,0:T(8,128)(2,1)}) custom-call(f32[1,1]{1,0:T(1,128)S(6)} %copy.17.xs_in, s32[1,1]{1,0:T(1,128)S(6)} %copy.18.xo_in, f32[1,1]{1,0:T(1,128)S(6)} %copy.19.gs_in, s32[1,1]{1,0:T(1,128)S(6)} %copy.20.go_in, ...), custom_call_target="tpu_custom_call" | custom-call | flops 1200000000 | bytes 8000000 | tf_op jit(solution)/shard_map/ffn_backward/pallas_call | solution.py:433
  105.9 40.0 %deliver.1 = (bf16[24,128]{1,0:T(8,128)(2,1)}, bf16[128,1664]{1,0:T(8,128)(2,1)}, bf16[128,1664]{1,0:T(8,128)(2,1)}, bf16[1664,128]{1,0:T(8,128)(2,1)}) custom-call(bf16[24,128]{1,0:T(8,128)(2,1)} %get-tuple-element.8.a, bf16[128,1664]{1,0:T(8,128)(2,1)} %get-tuple-element.9.b, bf16[128,1664]{1,0:T(8,128)(2,1)} %get-tuple-element.10.c, ...), custom_call_target="tpu_custom_call" | custom-call | tf_op jit(solution)/shard_map/deliver/pallas_call | solution.py:416

commit v4 on v3

--- a/solution.py
+++ b/solution.py
@@ -53,7 +53,7 @@
         )
 
     barrier = pltpu.get_barrier_semaphore()
-    peers = [zdev(d) for d in (1, -1, 2, -2, STRIDE, -STRIDE)]
+    peers = [zdev(d) for d in (1, -1, 2, -2, 4, -4, 8, -8)]
     peers += [sib] + [tdev(i) for i in range(1, NT)]
     for peer in peers:
         pl.semaphore_signal(barrier, inc=1, device_id=peer, device_id_type=MESH)
@@ -94,20 +94,19 @@
         return lax.rem(z + d + NZ, NZ) // STRIDE
 
     class Gather:
-        def __init__(self, buf, ch, stride, towards, chain_s, chain_r, local_s, local_r):
+        def __init__(self, buf, ch, stride, towards, links, chain_s, chain_r, local_s, local_r):
             self.ch, self.stride, self.towards = ch, stride, towards
             self.nk = nk = NZ // stride
-            self.half = half = nk // 2
+            half = nk // 2
             self.which = tuple(range(0, -half - 1, -1)) + tuple(range(1, half))
 
             def slot(n):
                 return buf.at[self.rows(0, n)]
 
-            def link(n, at, d):
-                return rcopy(slot(n), slot(n), chain_s.at[at], chain_r.at[at], zdev(d))
-
-            self.right = [link(n, n, stride) for n in range(half)]
-            self.left = [link(half + n if n else 0, half + n, -stride) for n in range(half - 1)]
+            self.links = [
+                rcopy(slot(n), slot(n), chain_s.at[at], chain_r.at[at], zdev(d))
+                for at, (n, d) in enumerate(links)
+            ]
             self.local = []
             for n in range(nk):
                 if towards:
@@ -123,7 +122,7 @@
                     self.local.append(
                         [rcopy(slot(n), slot(n), local_s.at[n], local_r.at[at], to)]
                     )
-            self.all = self.right + self.left + sum(self.local, [])
+            self.all = self.links + sum(self.local, [])
 
         def index(self, d, n):
             return lax.rem(lax.rem(z + d + NZ, NZ) // self.stride + self.which[n] + self.nk, self.nk)
@@ -132,26 +131,14 @@
             cls_at = lax.rem(lax.rem(z, self.stride) + d + self.stride, self.stride)
             return rows_of(self.ch * (self.nk * cls_at + self.index(d, n)), self.ch)
 
-        def begin(self):
-            self.right[0].start()
-            self.left[0].start()
-            self.spread(0)
-
-        def spread(self, n):
-            for copy in self.local[n]:
-                copy.start()
-
-        def step(self, i):
-            half = self.half
-            self.right[i - 1].wait_recv()
-            if i < half:
-                self.right[i].start()
-                self.left[i - 1].wait_recv()
-            if i < half - 1:
-                self.left[i].start()
-            self.spread(i)
-            if i < half:
-                self.spread(half + i)
+        def send(self, *links):
+            for at in links:
+                self.links[at].start()
+
+        def spread(self, *chunks):
+            for n in chunks:
+                for copy in self.local[n]:
+                    copy.start()
 
         def arrive(self, n):
             for copy in self.local[n]:
@@ -163,7 +150,22 @@
         gpack[6 * j : 6 * j + 6, :] = gate_val[:, 128 * j : 128 * j + 128]
         gpack[CH + 6 * j : CH + 6 * j + 6, :] = up_val[:, 128 * j : 128 * j + 128]
 
-    saved = Gather(gbuf, GCH, 2, (), gch_s, gch_r, glo_s, glo_r)
+    saved = Gather(
+        gbuf, GCH, 2, (), [(n, 2) for n in range(8)] + [(8 + n if n else 0, -2) for n in range(7)],
+        gch_s, gch_r, glo_s, glo_r,
+    )
+
+    def saved_step(i):
+        saved.links[i - 1].wait_recv()
+        if i < 8:
+            saved.send(i)
+            saved.links[7 + i].wait_recv()
+        if i < 7:
+            saved.send(8 + i)
+        saved.spread(i)
+        if i < 8:
+            saved.spread(8 + i)
+
     gbuf[saved.rows(0, 0), :] = gpack[...].astype(BF16)
     pl.semaphore_wait(barrier, len(peers))
 
@@ -176,9 +178,10 @@
     wd_copy = rcopy(wd, wd2.at[:, pl.ds(128, 128)], sib_s.at[0], sib_r.at[0], sib)
     wd_copy.start()
 
-    saved.begin()
-
-    saved.step(1)
+    saved.send(0, 8)
+    saved.spread(0)
+
+    saved_step(1)
     for copy in xy:
         copy.wait_recv()
     for i in range(NT):
@@ -197,7 +200,7 @@
     loc[0].wait()
     wd_copy.wait_recv()
     og_copy.wait_recv()
-    saved.step(2)
+    saved_step(2)
 
     hp[J * ROWS : FLAT, :] = jnp.zeros((FLAT - J * ROWS, 128), BF16)
     hf[J * ROWS : FLAT, :] = jnp.zeros((FLAT - J * ROWS, 128), F32)
@@ -211,7 +214,7 @@
         hp[ROWS * j : ROWS * (j + 1), :] = val.astype(BF16)
 
     r1 = {}
-    for off in (4, 5, 3, 6, 2, 7, 1, 0):
+    for off in (4, 3, 5, 1, 7, 2, 6, 0):
         for n, d in enumerate((1, -1, 2)):
             base = CLS * near(d) + CH * lax.rem(k_of(d) + off, NK)
             r1[off, n] = rcopy(
@@ -226,33 +229,57 @@
             total = total + r1b[n, off].astype(F32)
         return total
 
-    saved.step(3)
-    r2 = {}
-    for i in range(1, 5):
-        for w, off, d in ((0, 5 - i, STRIDE), (1, 4 + i, -STRIDE)):
-            if w == 1 and i == 4:
-                continue
-            total = window_sum(off)
-            if i > 1:
-                r2[w, i - 1].wait_recv()
-                total = total + r2r[w, i - 2].astype(F32)
-            r2s[w, i - 1] = total.astype(BF16)
-            r2[w, i] = rcopy(
-                r2s.at[w, i - 1], r2r.at[w, i - 1], r2_s.at[w, i - 1], r2_r.at[w, i - 1], zdev(d)
-            )
-            r2[w, i].start()
-        saved.step(3 + i)
+    saved_step(3)
+    r2 = []
+
+    def pass_on(total, d):
+        m = len(r2)
+        r2s[m] = total.astype(BF16)
+        r2.append(rcopy(r2s.at[m], r2r.at[m], r2_s.at[m], r2_r.at[m], zdev(d)))
+        r2[m].start()
+
+    def passed(m):
+        r2[m].wait_recv()
+        return r2r[m].astype(F32)
+
+    pass_on(window_sum(4), 8)
+    pass_on(window_sum(3), 4)
+    pass_on(window_sum(5), -4)
+    saved_step(4)
+    pass_on(window_sum(1), 4)
+    pass_on(window_sum(7), -4)
+    saved_step(5)
+    right, left = window_sum(2), window_sum(6)
+    left = left + passed(2)
+    pass_on(left, -8)
+    right = right + passed(1)
+    right = right + passed(0)
+    pass_on(right, 8)
     total = window_sum(0)
-    r2[1, 3].wait_recv()
-    total = total + r2r[1, 2].astype(F32)
-    r2[0, 4].wait_recv()
-    total = total + r2r[0, 3].astype(F32)
-    back = Gather(ha, CH, STRIDE, (1, -1, -2), a1_s, a1_r, a2_s, a2_r)
+    total = total + passed(3)
+    total = total + passed(4)
+    saved_step(6)
+    total = total + passed(5)
+    total = total + passed(6)
+    back = Gather(
+        ha, CH, STRIDE, (1, -1, -2),
+        [(0, 4), (0, -4), (0, 8), (0, -8), (2, 4), (2, 8), (6, -4)],
+        a1_s, a1_r, a2_s, a2_r,
+    )
     ha[back.rows(0, 0), :] = total.astype(BF16)
-    back.begin()
-    saved.step(8)
-
-    back.step(1)
+    back.send(2, 3, 0, 1)
+    back.spread(0)
+    saved_step(7)
+    back.links[0].wait_recv()
+    back.links[1].wait_recv()
+    back.spread(1, 5)
+    saved_step(8)
+    back.links[2].wait_recv()
+    back.send(5, 4)
+    back.links[3].wait_recv()
+    back.send(6)
+    back.spread(2, 6)
+
     for n in range(NZ // 2):
         saved.arrive(n)
     coef_a[J * ROWS : FLAT, :] = jnp.zeros((FLAT - J * ROWS, 128), F32)
@@ -298,11 +325,11 @@
             back.local[n][m].wait_recv()
             grads(-d, n)
 
-    grads(0, 0)
-    for n in (1, 5):
+    for n in (0, 1, 5, 2, 6):
         grads(0, n)
     arrived(0)
-    back.step(2)
+    arrived(1)
+    arrived(5)
     hid_copy.wait_recv()
 
     def down(j, _):
@@ -319,16 +346,16 @@
     outs = [pltpu.make_async_copy(o_down, ddown, loc_sem.at[3])]
     outs[0].start()
 
-    grads(0, 2)
-    grads(0, 6)
-    arrived(1)
-    arrived(5)
-    back.step(3)
+    back.links[4].wait_recv()
+    back.spread(3)
+    back.links[6].wait_recv()
+    back.spread(7)
     grads(0, 3)
     grads(0, 7)
     arrived(2)
     arrived(6)
-    back.step(4)
+    back.links[5].wait_recv()
+    back.spread(4)
     grads(0, 4)
     arrived(3)
     arrived(7)
@@ -379,7 +406,7 @@
     outs[2].start()
 
     sends = xy + [wd_copy, og_copy, hid_copy] + saved.all + back.all + gu
-    sends += list(r1.values()) + list(r2.values())
+    sends += list(r1.values()) + r2
     for copy in sends:
         copy.wait_send()
     for copy in rs:
@@ -400,14 +427,17 @@
         copy.wait()
 
 
-def deliver_kernel(a, b, c, d, a_out, b_out, c_out, d_out, sem):
-    copies = [
-        pltpu.make_async_copy(src, dst, sem.at[n])
-        for n, (src, dst) in enumerate(((b, b_out), (c, c_out), (d, d_out), (a, a_out)))
-    ]
-    for copy in copies:
+def deliver_kernel(*refs):
+    srcs, dsts, bufs, sem = refs[:4], refs[4:8], refs[8:12], refs[12]
+    order = (1, 2, 3, 0)
+    ins = [pltpu.make_async_copy(srcs[n], bufs[n], sem.at[0, n]) for n in order]
+    outs = [pltpu.make_async_copy(bufs[n], dsts[n], sem.at[1, n]) for n in order]
+    for copy in ins:
         copy.start()
-    for copy in copies:
+    for n in range(4):
+        ins[n].wait()
+        outs[n].start()
+    for copy in outs:
         copy.wait()
 
 
@@ -419,7 +449,8 @@
         out_shape=tuple(jax.ShapeDtypeStruct(r.shape, r.dtype) for r in results),
         in_specs=[hbm] * 4,
         out_specs=(hbm,) * 4,
-        scratch_shapes=[pltpu.SemaphoreType.DMA((4,))],
+        scratch_shapes=[pltpu.VMEM(r.shape, r.dtype) for r in results]
+        + [pltpu.SemaphoreType.DMA((2, 4))],
         compiler_params=pltpu.CompilerParams(vmem_limit_bytes=63 * 1024 * 1024),
     )(*results)
 
@@ -467,8 +498,8 @@
             v((FLAT, 128), F32),
             v((FLAT, 128), BF16),
             v((3, NK, CH, 128), BF16),
-            v((2, 4, CH, 128), BF16),
-            v((2, 4, CH, 128), BF16),
+            v((7, CH, 128), BF16),
+            v((7, CH, 128), BF16),
             v((FLAT, 128), BF16),
             v((FLAT, 256), BF16),
             v((FLAT, 256), BF16),
@@ -486,7 +517,7 @@
             dma((NZ // 2 - 1,)), dma((NZ // 2 - 1,)),
             dma((NZ // 2,)), dma((NZ // 2,)),
             dma((3, NK)), dma((3, NK)),
-            dma((2, 4)), dma((2, 4)),
+            dma((7,)), dma((7,)),
             dma((NK - 1,)), dma((NK - 1,)),
             dma((3, NK)), dma((3, NK)),
             dma((NZ,)), dma((NZ,)),

time: 146 us -> 111 us (0.76)
  Pallas kernels: 143 us -> 107 us
    pallas_call x1, Pallas kernels: 40 us -> 2.12 us  [deliver(): pl.pallas_call(deliver_kernel, name='deliver', out_shape=tuple((jax.Shape...]
    pallas_call x1, Pallas kernels: 103 us -> 105 us  [on_device(): pl.pallas_call(kernel, name='ffn_backward', out_shape=(jax.ShapeDtypeStru...]
where the time goes in v4:
time: 111 us; the launch traced here: 110 us
  Pallas kernels  107 us (96%)
  between operations  3.22 us (3%)
    pallas_call x1, Pallas kernels, on_device(): pl.pallas_call(kernel, name='ffn_backward', out_shape=(jax.ShapeDtypeStru...  105 us

profile of v4, /device:TPU:1, one launch (start us, length us, event | category | flops | bytes accessed | tf_op | source)
XLA Modules:
  0.0 110.3 jit_solution(4660626540226189310)
XLA Ops:
  3.2 105.0 %ffn_backward.1 = (bf16[24,128]{1,0:T(8,128)(2,1)}, bf16[128,1664]{1,0:T(8,128)(2,1)}, bf16[128,1664]{1,0:T(8,128)(2,1)}, bf16[1664,128]{1,0:T(8,128)(2,1)}) custom-call(f32[1,1]{1,0:T(1,128)S(6)} %copy.17.xs_in, s32[1,1]{1,0:T(1,128)S(6)} %copy.18.xo_in, f32[1,1]{1,0:T(1,128)S(6)} %copy.19.gs_in, s32[1,1]{1,0:T(1,128)S(6)} %copy.20.go_in, ...), custom_call_target="tpu_custom_call" | custom-call | flops 1200000000 | bytes 8000000 | tf_op jit(solution)/shard_map/ffn_backward/pallas_call | solution.py:464
  108.2 2.1 %deliver.1 = (bf16[24,128]{1,0:T(8,128)(2,1)}, bf16[128,1664]{1,0:T(8,128)(2,1)}, bf16[128,1664]{1,0:T(8,128)(2,1)}, bf16[1664,128]{1,0:T(8,128)(2,1)}) custom-call(bf16[24,128]{1,0:T(8,128)(2,1)} %get-tuple-element.8.refs_0_, bf16[128,1664]{1,0:T(8,128)(2,1)} %get-tuple-element.9.refs_1_, bf16[128,1664]{1,0:T(8,128)(2,1)} %get-tuple-element.10.refs_2_, ...), custom_call_target="tpu_custom_call" | custom-call | tf_op jit(solution)/shard_map/deliver/pallas_call | solution.py:446

commit v5 on v3

--- a/solution.py
+++ b/solution.py
@@ -108,14 +108,21 @@
 
             self.right = [link(n, n, stride) for n in range(half)]
             self.left = [link(half + n if n else 0, half + n, -stride) for n in range(half - 1)]
-            self.local = []
+            self.local, self.across = [], []
             for n in range(nk):
                 if towards:
+                    odd = lax.rem(self.index(0, n), 2)
+                    to = (lax.rem(dp + 8 * odd - 4 + 2 * NZ, 2 * NZ), t)
+                    at = lax.rem(self.which[n] + 2 * nk - odd, nk)
                     self.local.append(
                         [
                             rcopy(slot(n), slot(n), local_s.at[m, n], local_r.at[m, n], zdev(d))
                             for m, d in enumerate(towards)
                         ]
+                        + [rcopy(slot(n), slot(n), local_s.at[2, n], local_r.at[2, at], to)]
+                    )
+                    self.across.append(
+                        rcopy(slot(n), slot(n), local_s.at[2, n], local_r.at[2, self.which[n] % nk], to)
                     )
                 else:
                     at = self.index(0, n)
@@ -210,19 +217,24 @@
         hf[ROWS * j : ROWS * (j + 1), :] = val
         hp[ROWS * j : ROWS * (j + 1), :] = val.astype(BF16)
 
-    r1 = {}
+    r1, r1_in = {}, {}
     for off in (4, 5, 3, 6, 2, 7, 1, 0):
         for n, d in enumerate((1, -1, 2)):
-            base = CLS * near(d) + CH * lax.rem(k_of(d) + off, NK)
-            r1[off, n] = rcopy(
-                hp.at[rows_of(base, CH)], r1b.at[n, off], r1_s.at[n, off], r1_r.at[n, off], zdev(d)
-            )
+            k = lax.rem(k_of(d) + off, NK)
+            to, at = zdev(d), off
+            if n == 2:
+                odd = lax.rem(k, 2)
+                to = (lax.rem(dp + 4 - 8 * odd + 2 * NZ, 2 * NZ), t)
+                at = lax.rem(off + odd, NK)
+            src = hp.at[rows_of(CLS * near(d) + CH * k, CH)]
+            r1[off, n] = rcopy(src, r1b.at[n, at], r1_s.at[n, off], r1_r.at[n, at], to)
+            r1_in[off, n] = rcopy(src, r1b.at[n, off], r1_s.at[n, off], r1_r.at[n, off], to)
             r1[off, n].start()
 
     def window_sum(off):
         total = hf[rows_of(CLS * cls + CH * lax.rem(k0 + off, NK), CH), :]
         for n in range(3):
-            r1[off, n].wait_recv()
+            r1_in[off, n].wait_recv()
             total = total + r1b[n, off].astype(F32)
         return total
 
@@ -247,7 +259,7 @@
     total = total + r2r[1, 2].astype(F32)
     r2[0, 4].wait_recv()
     total = total + r2r[0, 3].astype(F32)
-    back = Gather(ha, CH, STRIDE, (1, -1, -2), a1_s, a1_r, a2_s, a2_r)
+    back = Gather(ha, CH, STRIDE, (1, -1), a1_s, a1_r, a2_s, a2_r)
     ha[back.rows(0, 0), :] = total.astype(BF16)
     back.begin()
     saved.step(8)
@@ -297,6 +309,8 @@
         for m, d in enumerate(back.towards):
             back.local[n][m].wait_recv()
             grads(-d, n)
+        back.across[n].wait_recv()
+        grads(2, n)
 
     grads(0, 0)
     for n in (1, 5):
@@ -400,14 +414,17 @@
         copy.wait()
 
 
-def deliver_kernel(a, b, c, d, a_out, b_out, c_out, d_out, sem):
-    copies = [
-        pltpu.make_async_copy(src, dst, sem.at[n])
-        for n, (src, dst) in enumerate(((b, b_out), (c, c_out), (d, d_out), (a, a_out)))
-    ]
-    for copy in copies:
+def deliver_kernel(*refs):
+    srcs, dsts, bufs, sem = refs[:4], refs[4:8], refs[8:12], refs[12]
+    order = (1, 2, 3, 0)
+    ins = [pltpu.make_async_copy(srcs[n], bufs[n], sem.at[0, n]) for n in order]
+    outs = [pltpu.make_async_copy(bufs[n], dsts[n], sem.at[1, n]) for n in order]
+    for copy in ins:
         copy.start()
-    for copy in copies:
+    for n in range(4):
+        ins[n].wait()
+        outs[n].start()
+    for copy in outs:
         copy.wait()
 
 
@@ -419,7 +436,8 @@
         out_shape=tuple(jax.ShapeDtypeStruct(r.shape, r.dtype) for r in results),
         in_specs=[hbm] * 4,
         out_specs=(hbm,) * 4,
-        scratch_shapes=[pltpu.SemaphoreType.DMA((4,))],
+        scratch_shapes=[pltpu.VMEM(r.shape, r.dtype) for r in results]
+        + [pltpu.SemaphoreType.DMA((2, 4))],
         compiler_params=pltpu.CompilerParams(vmem_limit_bytes=63 * 1024 * 1024),
     )(*results)
 

time: 146 us -> 107 us (0.73)
  Pallas kernels: 143 us -> 103 us
    pallas_call x1, Pallas kernels: 40 us -> 2.12 us  [deliver(): pl.pallas_call(deliver_kernel, name='deliver', out_shape=tuple((jax.Shape...]
    pallas_call x1, Pallas kernels: 103 us -> 101 us  [on_device(): pl.pallas_call(kernel, name='ffn_backward', out_shape=(jax.ShapeDtypeStru...]
where the time goes in v5:
time: 107 us
  Pallas kernels  103 us (96%)
  between operations  3.22 us (3%)
    pallas_call x1, Pallas kernels, on_device(): pl.pallas_call(kernel, name='ffn_backward', out_shape=(jax.ShapeDtypeStru...  101 us

profile of v5, /device:TPU:1, one launch (start us, length us, event | category | flops | bytes accessed | tf_op | source)
XLA Modules:
  0.0 106.5 jit_solution(15840986700522275995)
XLA Ops:
  3.2 101.2 %ffn_backward.1 = (bf16[24,128]{1,0:T(8,128)(2,1)}, bf16[128,1664]{1,0:T(8,128)(2,1)}, bf16[128,1664]{1,0:T(8,128)(2,1)}, bf16[1664,128]{1,0:T(8,128)(2,1)}) custom-call(f32[1,1]{1,0:T(1,128)S(6)} %copy.17.xs_in, s32[1,1]{1,0:T(1,128)S(6)} %copy.18.xo_in, f32[1,1]{1,0:T(1,128)S(6)} %copy.19.gs_in, s32[1,1]{1,0:T(1,128)S(6)} %copy.20.go_in, ...), custom_call_target="tpu_custom_call" | custom-call | flops 1200000000 | bytes 8000000 | tf_op jit(solution)/shard_map/ffn_backward/pallas_call | solution.py:451
  104.4 2.1 %deliver.1 = (bf16[24,128]{1,0:T(8,128)(2,1)}, bf16[128,1664]{1,0:T(8,128)(2,1)}, bf16[128,1664]{1,0:T(8,128)(2,1)}, bf16[1664,128]{1,0:T(8,128)(2,1)}) custom-call(bf16[24,128]{1,0:T(8,128)(2,1)} %get-tuple-element.8.refs_0_, bf16[128,1664]{1,0:T(8,128)(2,1)} %get-tuple-element.9.refs_1_, bf16[128,1664]{1,0:T(8,128)(2,1)} %get-tuple-element.10.refs_2_, ...), custom_call_target="tpu_custom_call" | custom-call | tf_op jit(solution)/shard_map/deliver/pallas_call | solution.py:433
